TPU v7x, 32 devices: a whole 2x2x4 slice. The times are simulated.
32 devices in a mesh: row: 8 (over z, core), col: 4 (over y, x).
Axes of the slice: x: 2, y: 2, z: 4, core: 2. Of those that a mesh axis runs over, the one named last changes fastest.
Arguments:
- stress: float32 [256, 4096], P('col', 'row'), may hold values from -2.5 to 2.5
- state: float32 [256, 2048], P('col', 'row'), may hold values from 0 to 1
- load_rate: int32 [256, 4096], P('col', 'row'), may hold values from 0 to 2047
- a_param: float32 [2048], P('row'), may hold values from 1 to 2
- b_param: float32 [2048], P('row'), may hold values from 0.25 to 1
- near_band: bfloat16 [4096, 768], P('row'), may hold values from -0.21875 to 0.21875
- u_far: bfloat16 [16, 16, 32, 256], P('row', 'col'), may hold values from -0.375 to 0.375
- v_far: bfloat16 [16, 16, 32, 256], P('row', 'col'), may hold values from -0.375 to 0.375
- ranks: int32 [16, 16], P('row', 'col'), may hold values from 1 to 32, as said below
Outputs:
- new_stress: float32 [256, 4096], P('col', 'row')
- new_state: float32 [256, 2048], P('col', 'row')
Inputs may be any that keep to these rules, and one draw needn't show every extreme that they name: ranks of blocks with |I - J| <= 1 are not used; blocks with |I - J| = 2 have rank 32.
All inputs are finite; a program needn't handle non-finite values.
Results may differ from a plain program's by a relative error of at most 0.0021.
Values may be sent and summed in bfloat16 or wider, within the bound.
A program may use at most 64 MiB of HBM per device.

v0:
```python
import jax
import jax.numpy as jnp
from jax import lax
from jax.sharding import PartitionSpec as P

B = 128


HSTEP = 0.2
RATE_UNIT = 1.0 / 1024.0


def broadcast(value, axis, source):
    kept = jnp.where(lax.axis_index(axis) == source, value, 0).astype(value.dtype)
    return lax.psum(kept, axis)


def extended(cells, sides, width):
    for axis, dim in sides:
        count = lax.axis_size(axis)
        ends = count - 1
        head = lax.slice_in_dim(cells, 0, width, axis=dim)
        tail = lax.slice_in_dim(cells, cells.shape[dim] - width, cells.shape[dim], axis=dim)
        cells = jnp.concatenate(
            [
                lax.ppermute(tail, axis, [(i, (i + 1) % count) for i in range(ends)]),
                cells,
                lax.ppermute(head, axis, [((i + 1) % count, i) for i in range(ends)]),
            ],
            axis=dim,
        )
    return cells


def rates_and_drift(stress_now, state_now, plate_rate, a_param, b_param):
    members = stress_now.shape[0]
    block_count = a_param.shape[0] // B
    stress_view = stress_now.reshape(members, block_count, 2, B)
    state_view = state_now.reshape(members, block_count, 1, B)
    direct_view = a_param.reshape(1, block_count, 1, B)
    evolve_view = b_param.reshape(1, block_count, B)
    slip_rate = 2.0 * jnp.exp(-state_view) * jnp.sinh(stress_view / direct_view)
    slip_speed = jnp.sqrt(jnp.sum(slip_rate * slip_rate, axis=2))
    drift = evolve_view * (jnp.exp(-state_view[:, :, 0]) - slip_speed)
    excess = (slip_rate - plate_rate.reshape(members, block_count, 2, B)).astype(jnp.bfloat16)
    return (excess.reshape(members, -1), drift.reshape(members, -1))


def far_terms(columns, u_far, v_far, ranks, row_index, col_index):
    block_rows, block_cols, rank_slots, block_dofs = u_far.shape
    members = columns.shape[0]
    grid = columns.reshape(members, block_cols, block_dofs)
    weights = jnp.einsum("mjd,ijrd->ijmr", grid, v_far, preferred_element_type=jnp.float32)
    global_rows = row_index * block_rows + jnp.arange(block_rows, dtype=jnp.int32)
    global_cols = col_index * block_cols + jnp.arange(block_cols, dtype=jnp.int32)
    distant = jnp.abs(global_rows[:, None] - global_cols[None, :]) >= 2
    active = (jnp.arange(rank_slots, dtype=jnp.int32)[None, None, :] < ranks[:, :, None]) & distant[
        :, :, None
    ]
    weights = jnp.where(active[:, :, None, :], weights, 0.0).astype(jnp.bfloat16)
    partial_value = jnp.einsum("ijmr,ijrd->mid", weights, u_far, preferred_element_type=jnp.float32)
    return partial_value.reshape(members, -1)


def near_terms(padded, near_band):
    block_dofs = near_band.shape[1] // 3
    block_rows = near_band.shape[0] // block_dofs
    members = padded.shape[0]
    segment = padded
    segment = segment.reshape(members, block_rows + 2, block_dofs)
    windows = jnp.concatenate(
        [segment[:, 0:block_rows], segment[:, 1 : block_rows + 1], segment[:, 2 : block_rows + 2]],
        axis=2,
    )
    band_view = near_band.reshape(block_rows, block_dofs, 3 * block_dofs)
    nearby = jnp.einsum("mik,idk->mid", windows, band_view, preferred_element_type=jnp.float32)
    return nearby.reshape(members, -1)


def local(stress, state, load_rate, a_param, b_param, near_band, u_far, v_far, ranks):
    row_index = lax.axis_index("row")
    col_index = lax.axis_index("col")
    row_ratio = lax.axis_size("row") // lax.axis_size("col")
    block_dofs = near_band.shape[1] // 3
    plate_rate = load_rate.astype(jnp.float32) * RATE_UNIT
    stress_start, state_start = (stress, state)

    def tendency(stress_now, state_now):
        excess, drift = rates_and_drift(stress_now, state_now, plate_rate, a_param, b_param)
        all_members = lax.all_gather(excess, "col", axis=0, tiled=True)
        owners = []
        for offset in range(row_ratio):
            owners.append(broadcast(all_members, "row", row_ratio * col_index + offset))
        columns = jnp.concatenate(owners, axis=1)
        partial_value = far_terms(columns, u_far, v_far, ranks, row_index, col_index)
        totals = lax.psum_scatter(partial_value, "col", scatter_dimension=0, tiled=True)
        padded_rows = extended(excess, (("row", 1),), block_dofs)
        totals = totals + near_terms(padded_rows, near_band)
        return (-totals, drift)

    rate_one, drift_one = tendency(stress_start, state_start)
    stress_one = stress_start + HSTEP * rate_one
    state_one = state_start + HSTEP * drift_one
    rate_two, drift_two = tendency(stress_one, state_one)
    stress_two = 0.75 * stress_start + 0.25 * (stress_one + HSTEP * rate_two)
    state_two = 0.75 * state_start + 0.25 * (state_one + HSTEP * drift_two)
    rate_three, drift_three = tendency(stress_two, state_two)
    new_stress = stress_start / 3.0 + 2.0 / 3.0 * (stress_two + HSTEP * rate_three)
    new_state = state_start / 3.0 + 2.0 / 3.0 * (state_two + HSTEP * drift_three)
    return (new_stress, new_state)


def solution(mesh):
    return jax.shard_map(
        local,
        mesh=mesh,
        in_specs=(
            P("col", "row"),
            P("col", "row"),
            P("col", "row"),
            P("row"),
            P("row"),
            P("row", None),
            P("row", "col", None, None),
            P("row", "col", None, None),
            P("row", "col"),
        ),
        out_specs=(P("col", "row"), P("col", "row")),
        check_vma=False,
    )
```

profile of v0, /device:TPU:1, one launch (start us, length us, event | category | flops | bytes accessed | tf_op | source)
XLA Modules:
  0.0 301.2 jit_solution(3489569349786071228)
XLA Ops:
  9.4 7.8 %all_gather.9 = bf16[256,512]{1,0:T(8,128)(2,1)S(1)} all-gather(bf16[64,512]{1,0:T(8,128)(2,1)S(1)} %fusion.53), channel_id=1, replica_groups=mesh['row'=8,'col'=4] {'col'}, dimensions={0}, use_global_device_ids=true | all-gather | bytes 327680 | tf_op jit(solution)/shard_map/all_gather | solution.py:90
  18.9 56.2 %all-reduce.11.cloned.1.call-done = (bf16[256,512]{1,0:T(8,128)(2,1)}, bf16[256,512]{1,0:T(8,128)(2,1)}) async-done(((bf16[256,512]{1,0:T(8,128)(2,1)}, bf16[256,512]{1,0:T(8,128)(2,1)}), (bf16[256,512]{1,0:T(8,128)(2,1)}, bf16[256,512]{1,0:T(8,128)(2,1)})) %all-reduce.11.cloned.1.call-update) | async-done | bytes 524304 | tf_op jit(solution)/shard_map/psum | solution.py:15
  75.1 1.1 pad_maximum_fusion
  78.7 4.5 %collective-permute-start = (bf16[64,256]{1,0:T(8,128)(2,1)S(1)}, bf16[64,256]{1,0:T(8,128)(2,1)S(1)}, u32[]{:S(2)}, u32[]{:S(2)}) collective-permute-start(bf16[64,256]{1,0:T(8,128)(2,1)S(1)} %get-tuple-element.31), channel_id=1, source_target_pairs={{0,4},{4,8},{8,12},{12,16},{16,20},{20,24},{24,28},{1,5},{5,9},{9,... | collective-permute-start | bytes 98312 | tf_op jit(solution)/shard_map/ppermute | solution.py:26
  83.3 1.9 collective-permute-start.1
  87.0 1.5 collective-permute-done.1
  89.2 15.1 %reduce-scatter.4.cloned.1.call-done = f32[64,512]{1,0:T(8,128)} async-done(((f32[256,512]{1,0:T(8,128)}), f32[64,512]{1,0:T(8,128)}) %reduce-scatter.4.cloned.1.call-update) | async-done | bytes 131088 | tf_op jit(solution)/shard_map/reduce_scatter | solution.py:96
  104.2 1.1 fusion.52
  105.3 6.9 %all_gather.10 = bf16[256,512]{1,0:T(8,128)(2,1)S(1)} all-gather(bf16[64,512]{1,0:T(8,128)(2,1)S(1)} %get-tuple-element.10), channel_id=1, replica_groups=mesh['row'=8,'col'=4] {'col'}, dimensions={0}, use_global_device_ids=true | all-gather | bytes 327680 | tf_op jit(solution)/shard_map/all_gather | solution.py:90
  113.1 56.9 %all-reduce.9.cloned.1.call-done = (bf16[256,512]{1,0:T(8,128)(2,1)}, bf16[256,512]{1,0:T(8,128)(2,1)}) async-done(((bf16[256,512]{1,0:T(8,128)(2,1)}, bf16[256,512]{1,0:T(8,128)(2,1)}), (bf16[256,512]{1,0:T(8,128)(2,1)}, bf16[256,512]{1,0:T(8,128)(2,1)})) %all-reduce.9.cloned.1.call-update) | async-done | bytes 524304 | tf_op jit(solution)/shard_map/psum | solution.py:15
  169.9 1.1 pad_maximum_fusion.1
  173.0 4.5 %collective-permute-start.2 = (bf16[64,256]{1,0:T(8,128)(2,1)S(1)}, bf16[64,256]{1,0:T(8,128)(2,1)S(1)}, u32[]{:S(2)}, u32[]{:S(2)}) collective-permute-start(bf16[64,256]{1,0:T(8,128)(2,1)S(1)} %get-tuple-element.29), channel_id=1, source_target_pairs={{0,4},{4,8},{8,12},{12,16},{16,20},{20,24},{24,28},{1,5},{5,9},{9,... | collective-permute-start | bytes 98312 | tf_op jit(solution)/shard_map/ppermute | solution.py:26
  177.5 1.9 collective-permute-start.3
  180.5 2.2 collective-permute-done.3
  183.4 15.1 %reduce-scatter.6.cloned.1.call-done = f32[64,512]{1,0:T(8,128)} async-done(((f32[256,512]{1,0:T(8,128)}), f32[64,512]{1,0:T(8,128)}) %reduce-scatter.6.cloned.1.call-update) | async-done | bytes 131088 | tf_op jit(solution)/shard_map/reduce_scatter | solution.py:96
  198.5 1.1 fusion.51
  199.6 6.9 %all_gather.11 = bf16[256,512]{1,0:T(8,128)(2,1)S(1)} all-gather(bf16[64,512]{1,0:T(8,128)(2,1)S(1)} %get-tuple-element.8), channel_id=1, replica_groups=mesh['row'=8,'col'=4] {'col'}, dimensions={0}, use_global_device_ids=true | all-gather | bytes 327680 | tf_op jit(solution)/shard_map/all_gather | solution.py:90
  207.4 56.8 %all-reduce.7.cloned.1.call-done = (bf16[256,512]{1,0:T(8,128)(2,1)}, bf16[256,512]{1,0:T(8,128)(2,1)}) async-done(((bf16[256,512]{1,0:T(8,128)(2,1)}, bf16[256,512]{1,0:T(8,128)(2,1)}), (bf16[256,512]{1,0:T(8,128)(2,1)}, bf16[256,512]{1,0:T(8,128)(2,1)})) %all-reduce.7.cloned.1.call-update) | async-done | bytes 524304 | tf_op jit(solution)/shard_map/psum | solution.py:15
  264.2 1.1 pad_maximum_fusion.2
  267.9 4.5 %collective-permute-start.4 = (bf16[64,256]{1,0:T(8,128)(2,1)S(1)}, bf16[64,256]{1,0:T(8,128)(2,1)S(1)}, u32[]{:S(2)}, u32[]{:S(2)}) collective-permute-start(bf16[64,256]{1,0:T(8,128)(2,1)S(1)} %get-tuple-element.27), channel_id=1, source_target_pairs={{0,4},{4,8},{8,12},{12,16},{16,20},{20,24},{24,28},{1,5},{5,9},{9,... | collective-permute-start | bytes 98312 | tf_op jit(solution)/shard_map/ppermute | solution.py:26
  272.5 1.9 collective-permute-start.5
  275.1 3.0 collective-permute-done.5
  278.8 14.0 %reduce-scatter.8.cloned.1.call-done = f32[64,512]{1,0:T(8,128)} async-done(((f32[256,512]{1,0:T(8,128)}), f32[64,512]{1,0:T(8,128)}) %reduce-scatter.8.cloned.1.call-update) | async-done | bytes 131088 | tf_op jit(solution)/shard_map/reduce_scatter | solution.py:96
  292.8 1.6 multiply_add_fusion
  (100 shorter events, 18.1 us)
Async XLA Ops:
  7.2 81.6 %copy-start = (bf16[512,768]{1,0:T(8,128)(2,1)S(1)}, bf16[512,768]{1,0:T(8,128)(2,1)}, u32[]{:S(2)}) copy-start(bf16[512,768]{1,0:T(8,128)(2,1)} %param.14) | copy-start | bytes 2359300
  7.2 67.9 %all-reduce.11.cloned.1.call-start = ((), (), s32[]{:S(2)}) async-start(), calls=%async_computation.8 | async-start | bytes 1048576 | tf_op jit(solution)/shard_map/psum | solution.py:15
  8.3 0.9 copy-start.1
  8.3 1.0 copy-start.4
  8.4 0.7 copy-start.6
  18.0 86.2 %reduce-scatter.4.cloned.1.call-start = ((), (), s32[]{:S(2)}) async-start(), calls=%async_computation.3 | async-start | bytes 655360 | tf_op jit(solution)/shard_map/reduce_scatter | solution.py:96
  18.1 0.7 copy-start.8
  76.2 0.9 copy-start.2
  76.2 1.0 copy-start.3
  78.7 91.3 %all-reduce.9.cloned.1.call-start = ((), (), s32[]{:S(2)}) async-start(), calls=%async_computation.7 | async-start | bytes 1048576 | tf_op jit(solution)/shard_map/psum | solution.py:15
  78.7 8.3 %collective-permute-start = (bf16[64,256]{1,0:T(8,128)(2,1)S(1)}, bf16[64,256]{1,0:T(8,128)(2,1)S(1)}, u32[]{:S(2)}, u32[]{:S(2)}) collective-permute-start(bf16[64,256]{1,0:T(8,128)(2,1)S(1)} %get-tuple-element.31), channel_id=1, source_target_pairs={{0,4},{4,8},{8,12},{12,16},{16,20},{20,24},{24,28},{1,5},{5,9},{9,... | collective-permute-start | bytes 98312 | tf_op jit(solution)/shard_map/ppermute | solution.py:26
  83.3 5.2 %collective-permute-start.1 = (bf16[64,256]{1,0:T(8,128)(2,1)S(1)}, bf16[64,256]{1,0:T(8,128)(2,1)S(1)}, u32[]{:S(2)}, u32[]{:S(2)}) collective-permute-start(bf16[64,256]{1,0:T(8,128)(2,1)S(1)} %get-tuple-element.32), channel_id=1, source_target_pairs={{4,0},{8,4},{12,8},{16,12},{20,16},{24,20},{28,24},{5,1},{9,5},{13... | collective-permute-start | bytes 98312 | tf_op jit(solution)/shard_map/ppermute | solution.py:28
  85.9 0.8 copy-start.5
  86.0 0.8 copy-start.7
  113.0 85.5 %reduce-scatter.6.cloned.1.call-start = ((), (), s32[]{:S(2)}) async-start(), calls=%async_computation.4 | async-start | bytes 655360 | tf_op jit(solution)/shard_map/reduce_scatter | solution.py:96
  172.9 91.3 %all-reduce.7.cloned.1.call-start = ((), (), s32[]{:S(2)}) async-start(), calls=%async_computation.6 | async-start | bytes 1048576 | tf_op jit(solution)/shard_map/psum | solution.py:15
  173.0 7.5 %collective-permute-start.2 = (bf16[64,256]{1,0:T(8,128)(2,1)S(1)}, bf16[64,256]{1,0:T(8,128)(2,1)S(1)}, u32[]{:S(2)}, u32[]{:S(2)}) collective-permute-start(bf16[64,256]{1,0:T(8,128)(2,1)S(1)} %get-tuple-element.29), channel_id=1, source_target_pairs={{0,4},{4,8},{8,12},{12,16},{16,20},{20,24},{24,28},{1,5},{5,9},{9,... | collective-permute-start | bytes 98312 | tf_op jit(solution)/shard_map/ppermute | solution.py:26
  177.5 5.2 %collective-permute-start.3 = (bf16[64,256]{1,0:T(8,128)(2,1)S(1)}, bf16[64,256]{1,0:T(8,128)(2,1)S(1)}, u32[]{:S(2)}, u32[]{:S(2)}) collective-permute-start(bf16[64,256]{1,0:T(8,128)(2,1)S(1)} %get-tuple-element.30), channel_id=1, source_target_pairs={{4,0},{8,4},{12,8},{16,12},{20,16},{24,20},{28,24},{5,1},{9,5},{13... | collective-permute-start | bytes 98312 | tf_op jit(solution)/shard_map/ppermute | solution.py:28
  207.3 85.5 %reduce-scatter.8.cloned.1.call-start = ((), (), s32[]{:S(2)}) async-start(), calls=%async_computation.5 | async-start | bytes 655360 | tf_op jit(solution)/shard_map/reduce_scatter | solution.py:96
  267.9 7.2 %collective-permute-start.4 = (bf16[64,256]{1,0:T(8,128)(2,1)S(1)}, bf16[64,256]{1,0:T(8,128)(2,1)S(1)}, u32[]{:S(2)}, u32[]{:S(2)}) collective-permute-start(bf16[64,256]{1,0:T(8,128)(2,1)S(1)} %get-tuple-element.27), channel_id=1, source_target_pairs={{0,4},{4,8},{8,12},{12,16},{16,20},{20,24},{24,28},{1,5},{5,9},{9,... | collective-permute-start | bytes 98312 | tf_op jit(solution)/shard_map/ppermute | solution.py:26
  272.5 5.6 %collective-permute-start.5 = (bf16[64,256]{1,0:T(8,128)(2,1)S(1)}, bf16[64,256]{1,0:T(8,128)(2,1)S(1)}, u32[]{:S(2)}, u32[]{:S(2)}) collective-permute-start(bf16[64,256]{1,0:T(8,128)(2,1)S(1)} %get-tuple-element.28), channel_id=1, source_target_pairs={{4,0},{8,4},{12,8},{16,12},{20,16},{24,20},{28,24},{5,1},{9,5},{13... | collective-permute-start | bytes 98312 | tf_op jit(solution)/shard_map/ppermute | solution.py:28
Sparse Core Ops, SparseCore 0:
  18.2 56.8 all-reduce.10
  78.8 25.4 reduce-scatter.3
  113.1 56.7 all-reduce.8
  173.1 25.4 reduce-scatter.5
  207.4 56.7 all-reduce.6
  267.3 25.3 reduce-scatter.7
where the time goes:
time: 302 us; the launch traced here: 301 us
  waiting for transfers between devices  221 us (73%)
  blocking collectives  21.6 us (7%)
  starting transfers between devices  19.6 us (6%)
  between operations  14.7 us (5%)
  other arithmetic  13.4 us (4%)
  local copies, waits for them, and re-layouts  8.75 us (3%)
    psum x3, waiting for transfers between devices, broadcast(): return lax.psum(kept, axis)  170 us
    reduce_scatter x3, waiting for transfers between devices, tendency(): lax.psum_scatter(partial_value, 'col', scatter_dimension=0, tiled=True)  44.1 us
    all_gather x3, blocking collectives, tendency(): all_members = lax.all_gather(excess, 'col', axis=0, tiled=True)  21.6 us
    ppermute x3, starting transfers between devices, extended(): lax.ppermute(tail, axis, [(i, (i + 1) % count) for i in range(ends)])  13.6 us
    ppermute x3, waiting for transfers between devices, extended(): lax.ppermute(head, axis, [((i + 1) % count, i) for i in range(ends)])  6.68 us
  transfers between devices with their start and end apart: 12, of which 9 were waited for; matrix products, arithmetic and copies ran while one was open for 2% of the time, Pallas kernels for 0%

commit v1 on v0

v1 whole, which is shorter than its diff:
```python
import functools

import jax
import jax.numpy as jnp
from jax import lax
from jax.experimental import pallas as pl
from jax.experimental.pallas import tpu as pltpu
from jax.sharding import PartitionSpec as P

B = 128
HSTEP = 0.2
RATE_UNIT = 1.0 / 1024.0
MESH = pl.DeviceIdType.MESH


def partner(index, step, count):
    assert count & (count - 1) == 0
    bit = 1
    while bit <= step:
        if step & bit:
            index = index + bit - 2 * bit * ((index // bit) % 2)
        bit *= 2
    return index


def dot_t(left, right):
    return lax.dot_general(left, right, (((1,), (1,)), ((), ())), preferred_element_type=jnp.float32)


def kernel(
    rows,
    cols,
    stress_in,
    state_in,
    load_in,
    a_in,
    b_in,
    band_in,
    u_in,
    v_in,
    ranks,
    stress_out,
    state_out,
    stress0,
    state0,
    load,
    band,
    u_all,
    v_all,
    grid,
    load_sem,
    w_send,
    w_recv,
    g_send,
    g_recv,
    f_send,
    f_recv,
):
    row = lax.axis_index("row")
    col = lax.axis_index("col")
    chips = rows // 2
    chip = row // 2
    core = row % 2
    peer = 2 * chip + 1 - core
    _, block_rows, block_cols, slots, dofs = u_all.shape
    members = stress0.shape[0]

    barrier = pltpu.get_barrier_semaphore()
    others = [(row, partner(col, t, cols)) for t in range(1, cols)]
    others += [(2 * partner(chip, t, chips) + core, col) for t in range(1, chips)]
    others += [(peer, col)]
    for other in others:
        pl.semaphore_signal(barrier, inc=1, device_id=other, device_id_type=MESH)

    loads = [
        pltpu.make_async_copy(source, target, load_sem.at[n])
        for n, (source, target) in enumerate(
            [
                (u_in, u_all.at[col]),
                (stress_in, stress0),
                (state_in, state0),
                (load_in, load),
                (v_in, v_all.at[col]),
                (band_in, band),
            ]
        )
    ]
    for copy in loads:
        copy.start()

    loads[0].wait()
    slot = lax.broadcasted_iota(jnp.int32, (slots, dofs), 0)
    for i in range(block_rows):
        for j in range(block_cols):
            spacing = jnp.abs(row * block_rows + i - col * block_cols - j)
            limit = jnp.where(spacing >= 2, ranks[i, j], 0)
            factors = u_all[col, i, j].astype(jnp.float32)
            u_all[col, i, j] = jnp.where(slot < limit, factors, 0.0).astype(jnp.bfloat16)

    pl.semaphore_wait(barrier, len(others))

    def send(source, target, send_sem, recv_sem, device):
        copy = pltpu.make_async_remote_copy(
            src_ref=source,
            dst_ref=target,
            send_sem=send_sem,
            recv_sem=recv_sem,
            device_id=device,
            device_id_type=MESH,
        )
        copy.start()
        return copy

    col_steps = list(range(cols - 1, 0, -1))
    sent = []
    v_copies = {}
    for t in col_steps:
        v_copies[t] = send(
            v_in, v_all.at[col], w_send.at[0, t], w_recv.at[0, t], (row, partner(col, t, cols))
        )
    u_copies = {}

    def send_u():
        for t in col_steps:
            u_copies[t] = send(
                u_all.at[col], u_all.at[col], w_send.at[1, t], w_recv.at[1, t], (row, partner(col, t, cols))
            )

    def weights(s, j):
        parts = []
        per_row = block_cols // 2
        for n in range(block_cols):
            excess = grid[s, 2 * j + n // per_row, :, (n % per_row) * dofs : (n % per_row + 1) * dofs]
            factors = v_all[j, :, n].reshape(block_rows * slots, dofs)
            parts.append(dot_t(excess, factors).astype(jnp.bfloat16))
        return [
            jnp.concatenate([part[:, i * slots : (i + 1) * slots] for part in parts], axis=1)
            for i in range(block_rows)
        ]

    def far(j, weight):
        return [
            jnp.dot(
                weight[i], u_all[j, i].reshape(block_cols * slots, dofs), preferred_element_type=jnp.float32
            )
            for i in range(block_rows)
        ]

    def band_tile(i, n):
        return band[i * dofs : (i + 1) * dofs, n * dofs : (n + 1) * dofs]

    def section(s, stress_now, state_now):
        drift = []
        for i in range(block_rows):
            lanes = slice(i * B, (i + 1) * B)
            theta = state_now[:, lanes]
            direct = a_in[lanes].reshape(1, B)
            squares = None
            for d in range(2):
                dof = slice((2 * i + d) * B, (2 * i + d + 1) * B)
                scaled = stress_now[:, dof] / direct
                rate = jnp.exp(scaled - theta) - jnp.exp(-scaled - theta)
                plate = load[:, dof].astype(jnp.float32) * RATE_UNIT
                grid[s, row, :, dof] = (rate - plate).astype(jnp.bfloat16)
                squares = rate * rate if squares is None else squares + rate * rate
            drift.append((theta, squares, b_in[lanes].reshape(1, B)))
        mine = grid.at[s, row]
        order = list(range(2, chips)) + [1] if chips > 1 else []
        g_copies = {}
        f_copies = {0: send(mine, mine, f_send.at[s, 0], f_recv.at[s, 0], (peer, col))}
        for t in order:
            g_copies[t] = send(
                mine, mine, g_send.at[s, t], g_recv.at[s, t], (2 * partner(chip, t, chips) + core, col)
            )
        if s == 0:
            send_u()
            loads[4].wait()
            loads[5].wait()
        drift = jnp.concatenate(
            [evolve * (jnp.exp(-theta) - jnp.sqrt(squares)) for theta, squares, evolve in drift], axis=1
        )

        total = [None] * block_rows
        for i in range(block_rows):
            for n in range(max(i - 1, 0), min(i + 2, block_rows)):
                term = dot_t(grid[s, row, :, n * dofs : (n + 1) * dofs], band_tile(i, n - i + 1))
                total[i] = term if total[i] is None else total[i] + term

        def add(terms):
            for i in range(block_rows):
                total[i] = total[i] + terms[i]

        def relay(t):
            g_copies[t].wait_recv()
            got = grid.at[s, 2 * partner(chip, t, chips) + core]
            f_copies[t] = send(got, got, f_send.at[s, t], f_recv.at[s, t], (peer, col))

        f_copies[0].wait_recv()
        if s == 0:
            for t in range(1, chips):
                relay(t)
            for t in range(1, chips):
                f_copies[t].wait_recv()
            ready = [(col, weights(s, col))]
            for t in range(1, cols):
                v_copies[t].wait_recv()
                j = partner(col, t, cols)
                ready.append((j, weights(s, j)))
            for t, (j, weight) in enumerate(ready):
                if t > 0:
                    u_copies[t].wait_recv()
                add(far(j, weight))
        else:
            for t in range(1, chips):
                relay(t)
                if t > 1:
                    f_copies[t - 1].wait_recv()
                j = partner(chip, t - 1, chips)
                add(far(j, weights(s, j)))
            if chips > 1:
                f_copies[chips - 1].wait_recv()
            j = partner(chip, chips - 1, chips)
            add(far(j, weights(s, j)))

        left = grid[s, (row + rows - 1) % rows, :, (block_rows - 1) * dofs :]
        right = grid[s, (row + 1) % rows, :, :dofs]
        left_term = dot_t(left, band_tile(0, 0))
        right_term = dot_t(right, band_tile(block_rows - 1, 2))
        total[0] = total[0] + jnp.where(row > 0, left_term, 0.0)
        total[-1] = total[-1] + jnp.where(row < rows - 1, right_term, 0.0)
        sent.extend(g_copies.values())
        sent.extend(f_copies.values())
        return -jnp.concatenate(total, axis=1), drift

    for copy in loads[1:4]:
        copy.wait()
    rate, drift = section(0, stress0[...], state0[...])
    stress_out[...] = stress0[...] + HSTEP * rate
    state_out[...] = state0[...] + HSTEP * drift
    rate, drift = section(1, stress_out[...], state_out[...])
    stress_out[...] = 0.75 * stress0[...] + 0.25 * (stress_out[...] + HSTEP * rate)
    state_out[...] = 0.75 * state0[...] + 0.25 * (state_out[...] + HSTEP * drift)
    rate, drift = section(2, stress_out[...], state_out[...])
    stress_out[...] = stress0[...] / 3.0 + 2.0 / 3.0 * (stress_out[...] + HSTEP * rate)
    state_out[...] = state0[...] / 3.0 + 2.0 / 3.0 * (state_out[...] + HSTEP * drift)
    sent.extend(v_copies.values())
    sent.extend(u_copies.values())
    for copy in sent:
        copy.wait_send()


def local(stress, state, load_rate, a_param, b_param, near_band, u_far, v_far, ranks):
    rows = lax.axis_size("row")
    cols = lax.axis_size("col")
    members, own = stress.shape
    chips = rows // 2
    hbm = pl.BlockSpec(memory_space=pl.ANY)
    vmem = pl.BlockSpec(memory_space=pltpu.VMEM)
    smem = pl.BlockSpec(memory_space=pltpu.SMEM)
    dma = pltpu.SemaphoreType.DMA
    return pl.pallas_call(
        functools.partial(kernel, rows, cols),
        out_shape=(
            jax.ShapeDtypeStruct(stress.shape, jnp.float32),
            jax.ShapeDtypeStruct(state.shape, jnp.float32),
        ),
        in_specs=[hbm, hbm, hbm, vmem, vmem, hbm, hbm, hbm, smem],
        out_specs=(vmem, vmem),
        scratch_shapes=[
            pltpu.VMEM(stress.shape, jnp.float32),
            pltpu.VMEM(state.shape, jnp.float32),
            pltpu.VMEM(load_rate.shape, jnp.int32),
            pltpu.VMEM(near_band.shape, jnp.bfloat16),
            pltpu.VMEM((cols,) + u_far.shape, jnp.bfloat16),
            pltpu.VMEM((cols,) + v_far.shape, jnp.bfloat16),
            pltpu.VMEM((3, rows, members, own), jnp.bfloat16),
            dma((6,)),
            dma((2, cols)),
            dma((2, cols)),
            dma((3, chips)),
            dma((3, chips)),
            dma((3, chips)),
            dma((3, chips)),
        ],
        compiler_params=pltpu.CompilerParams(
            collective_id=0, has_side_effects=True, vmem_limit_bytes=48 * 1024 * 1024
        ),
        cost_estimate=pl.CostEstimate(flops=400_000_000, bytes_accessed=4_000_000, transcendentals=300_000),
    )(stress, state, load_rate, a_param, b_param, near_band, u_far, v_far, ranks)


def solution(mesh):
    return jax.shard_map(
        local,
        mesh=mesh,
        in_specs=(
            P("col", "row"),
            P("col", "row"),
            P("col", "row"),
            P("row"),
            P("row"),
            P("row", None),
            P("row", "col", None, None),
            P("row", "col", None, None),
            P("row", "col"),
        ),
        out_specs=(P("col", "row"), P("col", "row")),
        check_vma=False,
    )
```

time: 302 us -> 46 us (0.15)
  waiting for transfers between devices: 221 us -> 0 us
  Pallas kernels: 0 us -> 36.1 us
  blocking collectives: 21.6 us -> 0 us
  starting transfers between devices: 19.6 us -> 0 us
  between operations: 14.7 us -> 0.66 us
  other arithmetic: 13.4 us -> 0 us
    psum x3 -> x0, waiting for transfers between devices: 170 us -> none  [broadcast(): return lax.psum(kept, axis)]
    reduce_scatter x3 -> x0, waiting for transfers between devices: 44.1 us -> none  [tendency(): lax.psum_scatter(partial_value, 'col', scatter_dimension=0, tiled=True)]
    pallas_call x0 -> x1, Pallas kernels: none -> 36.1 us  [local(): pl.pallas_call(functools.partial(kernel, rows, cols), out_shape=(jax.Shap...]
    all_gather x3 -> x0, blocking collectives: 21.6 us -> none  [tendency(): all_members = lax.all_gather(excess, 'col', axis=0, tiled=True)]
    ppermute x6 -> x0, starting transfers between devices: 19.3 us -> none  [the longest x3 13.6 us: extended(): lax.ppermute(tail, axis, [(i, (i + 1) % count) for i in range(ends)])]
    ppermute x6 -> x0, waiting for transfers between devices: 6.69 us -> none  [the longest x3 6.68 us: extended(): lax.ppermute(head, axis, [((i + 1) % count, i) for i in range(ends)])]
    unnamed x27 -> x20, local copies, waits for them, and re-layouts: 2.87 us -> 8.9 us
    reshape x15 -> x0, local copies, waits for them, and re-layouts: 4.67 us -> none  [the longest x3 3.01 us: far_terms(): return partial_value.reshape(members, -1)]
  transfers between devices with their start and end apart: 12 -> 0, of which waited for: 9 -> 0; matrix products, arithmetic and copies ran while one was open for 2% -> 0% of each run, Pallas kernels for 0% -> 0%
where the time goes in v1:
time: 46 us; the launch traced here: 45.6 us
  Pallas kernels  36.1 us (78%)
  local copies, waits for them, and re-layouts  8.9 us (19%)
  between operations  0.66 us (1%)
    pallas_call x1, Pallas kernels, local(): pl.pallas_call(functools.partial(kernel, rows, cols), out_shape=(jax.Shap...  36.1 us
    unnamed x20, local copies, waits for them, and re-layouts  8.9 us

profile of v1, /device:TPU:1, one launch (start us, length us, event | category | flops | bytes accessed | tf_op | source)
XLA Modules:
  0.0 45.6 jit_solution(13246712951034128038)
XLA Ops:
  0.6 0.0 copy-start
  0.6 1.1 %copy-done = bf16[512,768]{1,0:T(8,128)(2,1)S(1)} copy-done((bf16[512,768]{1,0:T(8,128)(2,1)S(1)}, bf16[512,768]{1,0:T(8,128)(2,1)}, u32[]{:S(2)}) %copy-start) | copy-done | bytes 786456
  1.8 0.0 copy-start.1
  1.8 0.9 %copy-done.1 = f32[64,512]{1,0:T(8,128)S(1)} copy-done((f32[64,512]{1,0:T(8,128)S(1)}, f32[64,512]{1,0:T(8,128)}, u32[]{:S(2)}) %copy-start.1) | copy-done | bytes 131096
  2.7 0.0 copy-start.2
  2.7 0.9 %copy-done.2 = s32[64,512]{1,0:T(8,128)S(1)} copy-done((s32[64,512]{1,0:T(8,128)S(1)}, s32[64,512]{1,0:T(8,128)}, u32[]{:S(2)}) %copy-start.2) | copy-done | bytes 131096
  3.6 0.0 copy-start.3
  3.6 0.9 %copy-done.3 = bf16[2,4,32,256]{3,2,1,0:T(8,128)(2,1)S(1)} copy-done((bf16[2,4,32,256]{3,2,1,0:T(8,128)(2,1)S(1)}, bf16[2,4,32,256]{3,2,1,0:T(8,128)(2,1)}, u32[]{:S(2)}) %copy-start.3) | copy-done | bytes 131096
  4.5 0.0 copy-start.4
  4.5 0.9 %copy-done.4 = bf16[2,4,32,256]{3,2,1,0:T(8,128)(2,1)S(1)} copy-done((bf16[2,4,32,256]{3,2,1,0:T(8,128)(2,1)S(1)}, bf16[2,4,32,256]{3,2,1,0:T(8,128)(2,1)}, u32[]{:S(2)}) %copy-start.4) | copy-done | bytes 131096
  5.4 0.0 copy-start.5
  5.4 0.8 %copy-done.5 = f32[64,256]{1,0:T(8,128)S(1)} copy-done((f32[64,256]{1,0:T(8,128)S(1)}, f32[64,256]{1,0:T(8,128)}, u32[]{:S(2)}) %copy-start.5) | copy-done | bytes 65560
  6.2 0.0 copy-start.6
  6.2 0.7 %copy-done.6 = f32[256]{0:T(256)S(1)} copy-done((f32[256]{0:T(256)S(1)}, f32[256]{0:T(256)}, u32[]{:S(2)}) %copy-start.6) | copy-done | bytes 1048
  6.9 0.0 copy-start.7
  6.9 0.7 %copy-done.7 = f32[256]{0:T(256)S(1)} copy-done((f32[256]{0:T(256)S(1)}, f32[256]{0:T(256)}, u32[]{:S(2)}) %copy-start.7) | copy-done | bytes 1048
  7.6 0.0 copy-start.8
  7.6 0.7 %copy-done.8 = s32[2,4]{1,0:T(2,128)S(1)} copy-done((s32[2,4]{1,0:T(2,128)S(1)}, s32[2,4]{1,0:T(2,128)}, u32[]{:S(2)}) %copy-start.8) | copy-done | bytes 56
  8.3 36.1 %shard_map.104 = (f32[64,512]{1,0:T(8,128)S(1)}, f32[64,256]{1,0:T(8,128)S(1)}) custom-call(f32[64,512]{1,0:T(8,128)S(1)} %copy-done.1, f32[64,256]{1,0:T(8,128)S(1)} %copy-done.5, s32[64,512]{1,0:T(8,128)S(1)} %copy-done.2, f32[256]{0:T(256)S(1)} %copy-done.6, f32[256]{0:T(256)S(1)} %copy-done.7, bf16[512,768]{1,0:T(8,128)(2,1)S(1)} %copy-done, ...), custom_call_target="tpu_custom_call" | custom-call | flops 400000000 | bytes 4000000 | tf_op jit(solution)/shard_map/pallas_call | solution.py:261
  44.3 0.7 %copy.13 = f32[64,512]{1,0:T(8,128)} copy(f32[64,512]{1,0:T(8,128)S(1)} %get-tuple-element.4) | data formatting | bytes 262144
  45.0 0.6 %copy.14 = f32[64,256]{1,0:T(8,128)} copy(f32[64,256]{1,0:T(8,128)S(1)} %get-tuple-element.5) | data formatting | bytes 131072
Async XLA Ops:
  0.6 1.1 %copy-start = (bf16[512,768]{1,0:T(8,128)(2,1)S(1)}, bf16[512,768]{1,0:T(8,128)(2,1)}, u32[]{:S(2)}) copy-start(bf16[512,768]{1,0:T(8,128)(2,1)} %band_in.1) | copy-start | bytes 2359300
  1.8 0.9 %copy-start.1 = (f32[64,512]{1,0:T(8,128)S(1)}, f32[64,512]{1,0:T(8,128)}, u32[]{:S(2)}) copy-start(f32[64,512]{1,0:T(8,128)} %stress_in.1) | copy-start | bytes 393220
  2.7 0.9 %copy-start.2 = (s32[64,512]{1,0:T(8,128)S(1)}, s32[64,512]{1,0:T(8,128)}, u32[]{:S(2)}) copy-start(s32[64,512]{1,0:T(8,128)} %load_in.1) | copy-start | bytes 393220
  3.6 0.9 %copy-start.3 = (bf16[2,4,32,256]{3,2,1,0:T(8,128)(2,1)S(1)}, bf16[2,4,32,256]{3,2,1,0:T(8,128)(2,1)}, u32[]{:S(2)}) copy-start(bf16[2,4,32,256]{3,2,1,0:T(8,128)(2,1)} %u_in.1) | copy-start | bytes 393220
  4.5 0.9 %copy-start.4 = (bf16[2,4,32,256]{3,2,1,0:T(8,128)(2,1)S(1)}, bf16[2,4,32,256]{3,2,1,0:T(8,128)(2,1)}, u32[]{:S(2)}) copy-start(bf16[2,4,32,256]{3,2,1,0:T(8,128)(2,1)} %v_in.1) | copy-start | bytes 393220
  5.4 0.8 %copy-start.5 = (f32[64,256]{1,0:T(8,128)S(1)}, f32[64,256]{1,0:T(8,128)}, u32[]{:S(2)}) copy-start(f32[64,256]{1,0:T(8,128)} %state_in.1) | copy-start | bytes 196612
  6.2 0.7 %copy-start.6 = (f32[256]{0:T(256)S(1)}, f32[256]{0:T(256)}, u32[]{:S(2)}) copy-start(f32[256]{0:T(256)} %a_in.1) | copy-start | bytes 3076
  6.9 0.7 %copy-start.7 = (f32[256]{0:T(256)S(1)}, f32[256]{0:T(256)}, u32[]{:S(2)}) copy-start(f32[256]{0:T(256)} %b_in.1) | copy-start | bytes 3076
  7.6 0.7 %copy-start.8 = (s32[2,4]{1,0:T(2,128)S(1)}, s32[2,4]{1,0:T(2,128)}, u32[]{:S(2)}) copy-start(s32[2,4]{1,0:T(2,128)} %ranks.1) | copy-start | bytes 100

commit v2 on v1

--- a/solution.py
+++ b/solution.py
@@ -33,17 +33,20 @@
     stress_in,
     state_in,
     load_in,
-    a_in,
-    b_in,
+    a_hbm,
+    b_hbm,
     band_in,
     u_in,
     v_in,
-    ranks,
+    ranks_hbm,
     stress_out,
     state_out,
     stress0,
     state0,
     load,
+    a_in,
+    b_in,
+    ranks,
     band,
     u_all,
     v_all,
@@ -66,7 +69,7 @@
     members = stress0.shape[0]
 
     barrier = pltpu.get_barrier_semaphore()
-    others = [(row, partner(col, t, cols)) for t in range(1, cols)]
+    others = [(row, partner(col, t, cols)) for t in ([1, 2] if cols == 4 else range(1, cols))]
     others += [(2 * partner(chip, t, chips) + core, col) for t in range(1, chips)]
     others += [(peer, col)]
     for other in others:
@@ -76,9 +79,12 @@
         pltpu.make_async_copy(source, target, load_sem.at[n])
         for n, (source, target) in enumerate(
             [
+                (ranks_hbm, ranks),
                 (u_in, u_all.at[col]),
                 (stress_in, stress0),
                 (state_in, state0),
+                (a_hbm, a_in),
+                (b_hbm, b_in),
                 (load_in, load),
                 (v_in, v_all.at[col]),
                 (band_in, band),
@@ -89,6 +95,7 @@
         copy.start()
 
     loads[0].wait()
+    loads[1].wait()
     slot = lax.broadcasted_iota(jnp.int32, (slots, dofs), 0)
     for i in range(block_rows):
         for j in range(block_cols):
@@ -111,20 +118,38 @@
         copy.start()
         return copy
 
-    col_steps = list(range(cols - 1, 0, -1))
     sent = []
-    v_copies = {}
-    for t in col_steps:
-        v_copies[t] = send(
-            v_in, v_all.at[col], w_send.at[0, t], w_recv.at[0, t], (row, partner(col, t, cols))
-        )
+    relayed = cols == 4
+    col_steps = [1, 2] if relayed else list(range(1, cols))
+
+    def send_factors(kind, source, owner, t, to):
+        target = (v_all, u_all)[kind].at[owner]
+        copy = send(source, target, w_send.at[kind, t], w_recv.at[kind, t], (row, partner(col, to, cols)))
+        sent.append(copy)
+        return copy
+
+    v_copies = {t: send_factors(0, v_in, col, t, t) for t in col_steps}
     u_copies = {}
 
     def send_u():
         for t in col_steps:
-            u_copies[t] = send(
-                u_all.at[col], u_all.at[col], w_send.at[1, t], w_recv.at[1, t], (row, partner(col, t, cols))
-            )
+            u_copies[t] = send_factors(1, u_all.at[col], col, t, t)
+
+    def relay_v():
+        if relayed:
+            v_copies[1].wait_recv()
+            owner = partner(col, 1, cols)
+            v_copies[3] = send_factors(0, v_all.at[owner], owner, 3, 2)
+
+    def relay_u():
+        if relayed:
+            u_copies[2].wait_recv()
+            owner = partner(col, 2, cols)
+            u_copies[3] = send_factors(1, u_all.at[owner], owner, 3, 1)
+
+    def wait_factors(copies, t):
+        if not (relayed and t == (1 if copies is v_copies else 2)):
+            copies[t].wait_recv()
 
     def weights(s, j):
         parts = []
@@ -173,9 +198,10 @@
                 mine, mine, g_send.at[s, t], g_recv.at[s, t], (2 * partner(chip, t, chips) + core, col)
             )
         if s == 0:
+            relay_v()
             send_u()
-            loads[4].wait()
-            loads[5].wait()
+            loads[7].wait()
+            loads[8].wait()
         drift = jnp.concatenate(
             [evolve * (jnp.exp(-theta) - jnp.sqrt(squares)) for theta, squares, evolve in drift], axis=1
         )
@@ -201,14 +227,15 @@
                 relay(t)
             for t in range(1, chips):
                 f_copies[t].wait_recv()
+            relay_u()
             ready = [(col, weights(s, col))]
             for t in range(1, cols):
-                v_copies[t].wait_recv()
+                wait_factors(v_copies, t)
                 j = partner(col, t, cols)
                 ready.append((j, weights(s, j)))
             for t, (j, weight) in enumerate(ready):
                 if t > 0:
-                    u_copies[t].wait_recv()
+                    wait_factors(u_copies, t)
                 add(far(j, weight))
         else:
             for t in range(1, chips):
@@ -232,7 +259,7 @@
         sent.extend(f_copies.values())
         return -jnp.concatenate(total, axis=1), drift
 
-    for copy in loads[1:4]:
+    for copy in loads[2:7]:
         copy.wait()
     rate, drift = section(0, stress0[...], state0[...])
     stress_out[...] = stress0[...] + HSTEP * rate
@@ -243,8 +270,6 @@
     rate, drift = section(2, stress_out[...], state_out[...])
     stress_out[...] = stress0[...] / 3.0 + 2.0 / 3.0 * (stress_out[...] + HSTEP * rate)
     state_out[...] = state0[...] / 3.0 + 2.0 / 3.0 * (state_out[...] + HSTEP * drift)
-    sent.extend(v_copies.values())
-    sent.extend(u_copies.values())
     for copy in sent:
         copy.wait_send()
 
@@ -254,9 +279,8 @@
     cols = lax.axis_size("col")
     members, own = stress.shape
     chips = rows // 2
-    hbm = pl.BlockSpec(memory_space=pl.ANY)
+    hbm = pl.BlockSpec(memory_space=pltpu.HBM)
     vmem = pl.BlockSpec(memory_space=pltpu.VMEM)
-    smem = pl.BlockSpec(memory_space=pltpu.SMEM)
     dma = pltpu.SemaphoreType.DMA
     return pl.pallas_call(
         functools.partial(kernel, rows, cols),
@@ -264,17 +288,20 @@
             jax.ShapeDtypeStruct(stress.shape, jnp.float32),
             jax.ShapeDtypeStruct(state.shape, jnp.float32),
         ),
-        in_specs=[hbm, hbm, hbm, vmem, vmem, hbm, hbm, hbm, smem],
+        in_specs=[hbm] * 9,
         out_specs=(vmem, vmem),
         scratch_shapes=[
             pltpu.VMEM(stress.shape, jnp.float32),
             pltpu.VMEM(state.shape, jnp.float32),
             pltpu.VMEM(load_rate.shape, jnp.int32),
+            pltpu.VMEM(a_param.shape, jnp.float32),
+            pltpu.VMEM(b_param.shape, jnp.float32),
+            pltpu.SMEM(ranks.shape, jnp.int32),
             pltpu.VMEM(near_band.shape, jnp.bfloat16),
             pltpu.VMEM((cols,) + u_far.shape, jnp.bfloat16),
             pltpu.VMEM((cols,) + v_far.shape, jnp.bfloat16),
             pltpu.VMEM((3, rows, members, own), jnp.bfloat16),
-            dma((6,)),
+            dma((9,)),
             dma((2, cols)),
             dma((2, cols)),
             dma((3, chips)),
@@ -283,7 +310,7 @@
             dma((3, chips)),
         ],
         compiler_params=pltpu.CompilerParams(
-            collective_id=0, has_side_effects=True, vmem_limit_bytes=48 * 1024 * 1024
+            collective_id=0, has_side_effects=True, vmem_limit_bytes=60 * 1024 * 1024
         ),
         cost_estimate=pl.CostEstimate(flops=400_000_000, bytes_accessed=4_000_000, transcendentals=300_000),
     )(stress, state, load_rate, a_param, b_param, near_band, u_far, v_far, ranks)

time: 46 us -> 40.3 us (0.88)
  local copies, waits for them, and re-layouts: 8.9 us -> 2.23 us
  Pallas kernels: 36.1 us -> 37.2 us
    unnamed x20 -> x4, local copies, waits for them, and re-layouts: 8.9 us -> 2.23 us
    pallas_call x1, Pallas kernels: 36.1 us -> 37.2 us  [local(): pl.pallas_call(functools.partial(kernel, rows, cols), out_shape=(jax.Shap...]
where the time goes in v2:
time: 40.3 us; the launch traced here: 40.1 us
  Pallas kernels  37.2 us (92%)
  local copies, waits for them, and re-layouts  2.23 us (6%)
  between operations  0.65 us (2%)
    pallas_call x1, Pallas kernels, local(): pl.pallas_call(functools.partial(kernel, rows, cols), out_shape=(jax.Shap...  37.2 us
    unnamed x4, local copies, waits for them, and re-layouts  2.23 us

profile of v2, /device:TPU:1, one launch (start us, length us, event | category | flops | bytes accessed | tf_op | source)
XLA Modules:
  0.0 40.1 jit_solution(1092710086263422333)
XLA Ops:
  0.6 37.2 %shard_map.104 = (f32[64,512]{1,0:T(8,128)}, f32[64,256]{1,0:T(8,128)}) custom-call(f32[64,512]{1,0:T(8,128)} %stress_in.1, f32[64,256]{1,0:T(8,128)} %state_in.1, s32[64,512]{1,0:T(8,128)} %load_in.1, f32[256]{0:T(256)} %a_hbm.1, f32[256]{0:T(256)} %b_hbm.1, bf16[512,768]{1,0:T(8,128)(2,1)} %band_in.1, bf16[2,4,32,256]{3,2,1,0:T(8,128)(2,1)} %u_in.1, ...), custom_call_target="tpu_custom_call" | custom-call | flops 400000000 | bytes 4000000 | tf_op jit(solution)/shard_map/pallas_call | solution.py:285
  37.9 0.0 copy-start
  37.9 1.6 %copy.13 = f32[64,512]{1,0:T(8,128)} copy(f32[64,512]{1,0:T(8,128)} %get-tuple-element.4) | data formatting | bytes 262144
  39.5 0.0 copy-done
  39.5 0.6 %copy.14 = f32[64,256]{1,0:T(8,128)} copy(f32[64,256]{1,0:T(8,128)S(1)} %copy-done) | data formatting | bytes 131072
Async XLA Ops:
  37.9 1.6 %copy-start = (f32[64,256]{1,0:T(8,128)S(1)}, f32[64,256]{1,0:T(8,128)}, u32[]{:S(2)}) copy-start(f32[64,256]{1,0:T(8,128)} %get-tuple-element.5) | copy-start | bytes 196612

commit v3 on v2

v3 whole, which is shorter than its diff:
```python
import functools

import jax
import jax.numpy as jnp
from jax import lax
from jax.experimental import pallas as pl
from jax.experimental.pallas import tpu as pltpu
from jax.sharding import PartitionSpec as P

B = 128
HSTEP = 0.2
RATE_UNIT = 1.0 / 1024.0
MESH = pl.DeviceIdType.MESH


def partner(index, step, count):
    assert count & (count - 1) == 0
    bit = 1
    while bit <= step:
        if step & bit:
            index = index + bit - 2 * bit * ((index // bit) % 2)
        bit *= 2
    return index


def kernel(
    rows,
    cols,
    stress_in,
    state_in,
    load_in,
    a_hbm,
    b_hbm,
    band_in,
    u_in,
    v_in,
    ranks_hbm,
    stress_out,
    state_out,
    stress0,
    state0,
    load,
    a_in,
    b_in,
    ranks,
    band,
    u_all,
    v_all,
    v_own,
    band_t,
    grid,
    load_sem,
    w_send,
    w_recv,
    g_send,
    g_recv,
    f_send,
    f_recv,
):
    row = lax.axis_index("row")
    col = lax.axis_index("col")
    chips = rows // 2
    chip = row // 2
    core = row % 2
    peer = 2 * chip + 1 - core
    _, block_rows, block_cols, slots, dofs = u_all.shape
    _, halves, _, half, _ = grid.shape

    barrier = pltpu.get_barrier_semaphore()
    others = [(row, partner(col, t, cols)) for t in ([1, 2] if cols == 4 else range(1, cols))]
    others += [(2 * partner(chip, t, chips) + core, col) for t in range(1, chips)]
    others += [(peer, col)]
    for other in others:
        pl.semaphore_signal(barrier, inc=1, device_id=other, device_id_type=MESH)

    loads = [
        pltpu.make_async_copy(source, target, load_sem.at[n])
        for n, (source, target) in enumerate(
            [
                (ranks_hbm, ranks),
                (v_in, v_own),
                (u_in, u_all.at[col]),
                (stress_in, stress0),
                (state_in, state0),
                (a_hbm, a_in),
                (b_hbm, b_in),
                (load_in, load),
                (band_in, band),
            ]
        )
    ]
    for copy in loads:
        copy.start()

    loads[1].wait()
    v_all[col] = v_own[...].reshape(block_rows * block_cols * slots, dofs).T

    pl.semaphore_wait(barrier, len(others))

    def send(source, target, send_sem, recv_sem, device):
        copy = pltpu.make_async_remote_copy(
            src_ref=source,
            dst_ref=target,
            send_sem=send_sem,
            recv_sem=recv_sem,
            device_id=device,
            device_id_type=MESH,
        )
        copy.start()
        return copy

    sent = []
    relayed = cols == 4
    col_steps = [1, 2] if relayed else list(range(1, cols))

    def send_factors(kind, source, owner, t, to):
        target = (v_all, u_all)[kind].at[owner]
        copy = send(source, target, w_send.at[kind, t], w_recv.at[kind, t], (row, partner(col, to, cols)))
        sent.append(copy)
        return copy

    v_copies = {t: send_factors(0, v_all.at[col], col, t, t) for t in col_steps}
    u_copies = {}

    def send_u():
        for t in col_steps:
            u_copies[t] = send_factors(1, u_all.at[col], col, t, t)

    def relay_v():
        if relayed:
            v_copies[1].wait_recv()
            owner = partner(col, 1, cols)
            v_copies[3] = send_factors(0, v_all.at[owner], owner, 3, 2)

    def relay_u():
        if relayed:
            u_copies[2].wait_recv()
            owner = partner(col, 2, cols)
            u_copies[3] = send_factors(1, u_all.at[owner], owner, 3, 1)

    def wait_factors(copies, t):
        if not (relayed and t == (1 if copies is v_copies else 2)):
            copies[t].wait_recv()

    def mask_u():
        loads[0].wait()
        loads[2].wait()
        slot = lax.broadcasted_iota(jnp.int32, (slots, dofs), 0)
        for i in range(block_rows):
            for j in range(block_cols):
                spacing = jnp.abs(row * block_rows + i - col * block_cols - j)
                limit = jnp.where(spacing >= 2, ranks[i, j], 0)
                factors = u_all[col, i, j].astype(jnp.float32)
                u_all[col, i, j] = jnp.where(slot < limit, factors, 0.0).astype(jnp.bfloat16)

    def weights(s, h, j):
        per_row = block_cols // 2
        blocks = [
            grid[s, h, 2 * j + n // per_row, :, (n % per_row) * dofs : (n % per_row + 1) * dofs]
            for n in range(block_cols)
        ]
        products = jnp.dot(
            jnp.concatenate(blocks, axis=0), v_all[j], preferred_element_type=jnp.float32
        )
        lane = lax.broadcasted_iota(jnp.int32, (half, block_rows * block_cols * slots), 1)
        owner = (lane // slots) % block_cols
        weight = products[:half]
        for n in range(1, block_cols):
            weight = jnp.where(owner == n, products[n * half : (n + 1) * half], weight)
        return weight.astype(jnp.bfloat16)

    def far(j, weight):
        width = block_cols * slots
        return [
            jnp.dot(
                weight[:, i * width : (i + 1) * width],
                u_all[j, i].reshape(width, dofs),
                preferred_element_type=jnp.float32,
            )
            for i in range(block_rows)
        ]

    def added(total, terms):
        return [old + term for old, term in zip(total, terms)]

    def near_own(s, h):
        total = [None] * block_rows
        for i in range(block_rows):
            for n in range(max(i - 1, 0), min(i + 2, block_rows)):
                term = jnp.dot(
                    grid[s, h, row, :, n * dofs : (n + 1) * dofs],
                    band_t[i, n - i + 1],
                    preferred_element_type=jnp.float32,
                )
                total[i] = term if total[i] is None else total[i] + term
        return total

    def near_edges(s, h, total):
        left = grid[s, h, (row + rows - 1) % rows, :, (block_rows - 1) * dofs :]
        right = grid[s, h, (row + 1) % rows, :, :dofs]
        left_term = jnp.dot(left, band_t[0, 0], preferred_element_type=jnp.float32)
        right_term = jnp.dot(right, band_t[block_rows - 1, 2], preferred_element_type=jnp.float32)
        total = list(total)
        total[0] = total[0] + jnp.where(row > 0, left_term, 0.0)
        total[-1] = total[-1] + jnp.where(row < rows - 1, right_term, 0.0)
        return total

    g_copies = {}
    f_copies = {}

    def stepped(s, start, now, rate):
        if s == 0:
            return start + HSTEP * rate
        if s == 1:
            return 0.75 * start + 0.25 * (now + HSTEP * rate)
        return start / 3.0 + 2.0 / 3.0 * (now + HSTEP * rate)

    def excess(s, h):
        members_now = slice(h * half, (h + 1) * half)
        stress_now, state_now = (stress0, state0) if s == 0 else (stress_out, state_out)
        later = []
        for i in range(block_rows):
            lanes = slice(i * B, (i + 1) * B)
            theta = state_now[members_now, lanes]
            direct = a_in[lanes].reshape(1, B)
            squares = None
            for d in range(2):
                dof = slice((2 * i + d) * B, (2 * i + d + 1) * B)
                scaled = stress_now[members_now, dof] / direct
                rate = jnp.exp(scaled - theta) - jnp.exp(-scaled - theta)
                plate = load[members_now, dof].astype(jnp.float32) * RATE_UNIT
                grid[s, h, row, :, dof] = (rate - plate).astype(jnp.bfloat16)
                squares = rate * rate if squares is None else squares + rate * rate
            later.append((lanes, theta, squares))
        mine = grid.at[s, h, row]
        f_copies[s, h, 0] = send(mine, mine, f_send.at[s, h, 0], f_recv.at[s, h, 0], (peer, col))
        for t in list(range(2, chips)) + list(range(1, min(2, chips))):
            g_copies[s, h, t] = send(
                mine,
                mine,
                g_send.at[s, h, t],
                g_recv.at[s, h, t],
                (2 * partner(chip, t, chips) + core, col),
            )
        for lanes, theta, squares in later:
            drift = b_in[lanes].reshape(1, B) * (jnp.exp(-theta) - jnp.sqrt(squares))
            state_out[members_now, lanes] = stepped(s, state0[members_now, lanes], theta, drift)

    def relay(s, h, t):
        g_copies[s, h, t].wait_recv()
        got = grid.at[s, h, 2 * partner(chip, t, chips) + core]
        f_copies[s, h, t] = send(got, got, f_send.at[s, h, t], f_recv.at[s, h, t], (peer, col))

    def finish(s, h, total):
        members_now = slice(h * half, (h + 1) * half)
        stress_now = stress0 if s == 0 else stress_out
        for i in range(block_rows):
            lanes = slice(i * dofs, (i + 1) * dofs)
            stress_out[members_now, lanes] = stepped(
                s, stress0[members_now, lanes], stress_now[members_now, lanes], -total[i]
            )

    for copy in loads[3:8]:
        copy.wait()
    for h in range(halves):
        excess(0, h)
    mask_u()
    relay_v()
    send_u()
    loads[8].wait()
    for i in range(block_rows):
        for n in range(3):
            band_t[i, n] = band[i * dofs : (i + 1) * dofs, n * dofs : (n + 1) * dofs].T
    for h in range(halves):
        for t in range(1, chips):
            relay(0, h, t)
    totals = [near_own(0, h) for h in range(halves)]
    for h in range(halves):
        for t in range(chips):
            f_copies[0, h, t].wait_recv()
        totals[h] = near_edges(0, h, totals[h])
    relay_u()
    ready = []
    for t in range(cols):
        j = partner(col, t, cols)
        if t > 0:
            wait_factors(v_copies, t)
        ready.append((j, [weights(0, h, j) for h in range(halves)]))
    for t, (j, weight) in enumerate(ready):
        if t > 0:
            wait_factors(u_copies, t)
        for h in range(halves):
            totals[h] = added(totals[h], far(j, weight[h]))
            if t == cols - 1:
                finish(0, h, totals[h])
                excess(1, h)

    for s in (1, 2):
        for h in range(halves):
            total = near_own(s, h)
            f_copies[s, h, 0].wait_recv()
            for t in range(1, chips):
                relay(s, h, t)
                if t > 1:
                    f_copies[s, h, t - 1].wait_recv()
                j = partner(chip, t - 1, chips)
                total = added(total, far(j, weights(s, h, j)))
            if chips > 1:
                f_copies[s, h, chips - 1].wait_recv()
            j = partner(chip, chips - 1, chips)
            total = added(total, far(j, weights(s, h, j)))
            finish(s, h, near_edges(s, h, total))
            if s == 1:
                excess(2, h)

    for copy in sent + list(g_copies.values()) + list(f_copies.values()):
        copy.wait_send()


def local(stress, state, load_rate, a_param, b_param, near_band, u_far, v_far, ranks):
    rows = lax.axis_size("row")
    cols = lax.axis_size("col")
    members, own = stress.shape
    block_rows, block_cols, slots, dofs = u_far.shape
    chips = rows // 2
    halves = 2 if members % 32 == 0 else 1
    hbm = pl.BlockSpec(memory_space=pltpu.HBM)
    vmem = pl.BlockSpec(memory_space=pltpu.VMEM)
    dma = pltpu.SemaphoreType.DMA
    return pl.pallas_call(
        functools.partial(kernel, rows, cols),
        out_shape=(
            jax.ShapeDtypeStruct(stress.shape, jnp.float32),
            jax.ShapeDtypeStruct(state.shape, jnp.float32),
        ),
        in_specs=[hbm] * 9,
        out_specs=(vmem, vmem),
        scratch_shapes=[
            pltpu.VMEM(stress.shape, jnp.float32),
            pltpu.VMEM(state.shape, jnp.float32),
            pltpu.VMEM(load_rate.shape, jnp.int32),
            pltpu.VMEM(a_param.shape, jnp.float32),
            pltpu.VMEM(b_param.shape, jnp.float32),
            pltpu.SMEM(ranks.shape, jnp.int32),
            pltpu.VMEM(near_band.shape, jnp.bfloat16),
            pltpu.VMEM((cols,) + u_far.shape, jnp.bfloat16),
            pltpu.VMEM((cols, dofs, block_rows * block_cols * slots), jnp.bfloat16),
            pltpu.VMEM(v_far.shape, jnp.bfloat16),
            pltpu.VMEM((block_rows, 3, dofs, dofs), jnp.bfloat16),
            pltpu.VMEM((3, halves, rows, members // halves, own), jnp.bfloat16),
            dma((9,)),
            dma((2, cols)),
            dma((2, cols)),
            dma((3, halves, chips)),
            dma((3, halves, chips)),
            dma((3, halves, chips)),
            dma((3, halves, chips)),
        ],
        compiler_params=pltpu.CompilerParams(
            collective_id=0, has_side_effects=True, vmem_limit_bytes=60 * 1024 * 1024
        ),
        cost_estimate=pl.CostEstimate(flops=400_000_000, bytes_accessed=4_000_000, transcendentals=300_000),
    )(stress, state, load_rate, a_param, b_param, near_band, u_far, v_far, ranks)


def solution(mesh):
    return jax.shard_map(
        local,
        mesh=mesh,
        in_specs=(
            P("col", "row"),
            P("col", "row"),
            P("col", "row"),
            P("row"),
            P("row"),
            P("row", None),
            P("row", "col", None, None),
            P("row", "col", None, None),
            P("row", "col"),
        ),
        out_specs=(P("col", "row"), P("col", "row")),
        check_vma=False,
    )
```

time: 40.3 us -> 39.6 us (0.983)
  Pallas kernels: 37.2 us -> 36.5 us
    pallas_call x1, Pallas kernels: 37.2 us -> 36.5 us  [local(): pl.pallas_call(functools.partial(kernel, rows, cols), out_shape=(jax.Shap...]
where the time goes in v3:
time: 39.6 us; the launch traced here: 39.3 us
  Pallas kernels  36.5 us (92%)
  local copies, waits for them, and re-layouts  2.23 us (6%)
  between operations  0.65 us (2%)
    pallas_call x1, Pallas kernels, local(): pl.pallas_call(functools.partial(kernel, rows, cols), out_shape=(jax.Shap...  36.5 us
    unnamed x4, local copies, waits for them, and re-layouts  2.23 us

profile of v3, /device:TPU:1, one launch (start us, length us, event | category | flops | bytes accessed | tf_op | source)
XLA Modules:
  0.0 39.3 jit_solution(17020005679809762070)
XLA Ops:
  0.6 36.5 %shard_map.104 = (f32[64,512]{1,0:T(8,128)}, f32[64,256]{1,0:T(8,128)}) custom-call(f32[64,512]{1,0:T(8,128)} %stress_in.1, f32[64,256]{1,0:T(8,128)} %state_in.1, s32[64,512]{1,0:T(8,128)} %load_in.1, f32[256]{0:T(256)} %a_hbm.1, f32[256]{0:T(256)} %b_hbm.1, bf16[512,768]{1,0:T(8,128)(2,1)} %band_in.1, bf16[2,4,32,256]{3,2,1,0:T(8,128)(2,1)} %u_in.1, ...), custom_call_target="tpu_custom_call" | custom-call | flops 400000000 | bytes 4000000 | tf_op jit(solution)/shard_map/pallas_call | solution.py:330
  37.1 0.0 copy-start
  37.1 1.6 %copy.13 = f32[64,512]{1,0:T(8,128)} copy(f32[64,512]{1,0:T(8,128)} %get-tuple-element.4) | data formatting | bytes 262144
  38.7 0.0 copy-done
  38.7 0.6 %copy.14 = f32[64,256]{1,0:T(8,128)} copy(f32[64,256]{1,0:T(8,128)S(1)} %copy-done) | data formatting | bytes 131072
Async XLA Ops:
  37.1 1.6 %copy-start = (f32[64,256]{1,0:T(8,128)S(1)}, f32[64,256]{1,0:T(8,128)}, u32[]{:S(2)}) copy-start(f32[64,256]{1,0:T(8,128)} %get-tuple-element.5) | copy-start | bytes 196612

commit v4 on v3

--- a/solution.py
+++ b/solution.py
@@ -207,6 +207,14 @@
 
     g_copies = {}
     f_copies = {}
+    left_for = set()
+    order = list(range(2, chips)) + list(range(1, min(2, chips)))
+
+    def leave(key):
+        if key not in left_for:
+            left_for.add(key)
+            for t in order:
+                g_copies[key + (t,)].wait_send()
 
     def stepped(s, start, now, rate):
         if s == 0:
@@ -215,7 +223,18 @@
             return 0.75 * start + 0.25 * (now + HSTEP * rate)
         return start / 3.0 + 2.0 / 3.0 * (now + HSTEP * rate)
 
-    def excess(s, h):
+    def spread(s, h):
+        mine = grid.at[s, h, row]
+        for t in order:
+            g_copies[s, h, t] = send(
+                mine,
+                mine,
+                g_send.at[s, h, t],
+                g_recv.at[s, h, t],
+                (2 * partner(chip, t, chips) + core, col),
+            )
+
+    def excess(s, h, at_once):
         members_now = slice(h * half, (h + 1) * half)
         stress_now, state_now = (stress0, state0) if s == 0 else (stress_out, state_out)
         later = []
@@ -234,14 +253,8 @@
             later.append((lanes, theta, squares))
         mine = grid.at[s, h, row]
         f_copies[s, h, 0] = send(mine, mine, f_send.at[s, h, 0], f_recv.at[s, h, 0], (peer, col))
-        for t in list(range(2, chips)) + list(range(1, min(2, chips))):
-            g_copies[s, h, t] = send(
-                mine,
-                mine,
-                g_send.at[s, h, t],
-                g_recv.at[s, h, t],
-                (2 * partner(chip, t, chips) + core, col),
-            )
+        if at_once:
+            spread(s, h)
         for lanes, theta, squares in later:
             drift = b_in[lanes].reshape(1, B) * (jnp.exp(-theta) - jnp.sqrt(squares))
             state_out[members_now, lanes] = stepped(s, state0[members_now, lanes], theta, drift)
@@ -263,7 +276,7 @@
     for copy in loads[3:8]:
         copy.wait()
     for h in range(halves):
-        excess(0, h)
+        excess(0, h, True)
     mask_u()
     relay_v()
     send_u()
@@ -272,7 +285,7 @@
         for n in range(3):
             band_t[i, n] = band[i * dofs : (i + 1) * dofs, n * dofs : (n + 1) * dofs].T
     for h in range(halves):
-        for t in range(1, chips):
+        for t in order:
             relay(0, h, t)
     totals = [near_own(0, h) for h in range(halves)]
     for h in range(halves):
@@ -293,27 +306,35 @@
             totals[h] = added(totals[h], far(j, weight[h]))
             if t == cols - 1:
                 finish(0, h, totals[h])
-                excess(1, h)
-
-    for s in (1, 2):
+                excess(1, h, h == 0)
+
+    turns = [(s, h) for s in (1, 2) for h in range(halves)]
+    for n, (s, h) in enumerate(turns):
+        total = near_own(s, h)
+        f_copies[s, h, 0].wait_recv()
+        behind = 0
+        for m, t in enumerate(order):
+            relay(s, h, t)
+            if halves > 1 and m == max(len(order) - 2, 0) and n + 1 < len(turns):
+                leave((s, h))
+                spread(*turns[n + 1])
+            if behind > 0:
+                f_copies[s, h, behind].wait_recv()
+            j = partner(chip, behind, chips)
+            total = added(total, far(j, weights(s, h, j)))
+            behind = t
+        if behind > 0:
+            f_copies[s, h, behind].wait_recv()
+        j = partner(chip, behind, chips)
+        total = added(total, far(j, weights(s, h, j)))
+        finish(s, h, near_edges(s, h, total))
+        if s == 1:
+            excess(2, h, halves == 1)
+
+    for s in range(3):
         for h in range(halves):
-            total = near_own(s, h)
-            f_copies[s, h, 0].wait_recv()
-            for t in range(1, chips):
-                relay(s, h, t)
-                if t > 1:
-                    f_copies[s, h, t - 1].wait_recv()
-                j = partner(chip, t - 1, chips)
-                total = added(total, far(j, weights(s, h, j)))
-            if chips > 1:
-                f_copies[s, h, chips - 1].wait_recv()
-            j = partner(chip, chips - 1, chips)
-            total = added(total, far(j, weights(s, h, j)))
-            finish(s, h, near_edges(s, h, total))
-            if s == 1:
-                excess(2, h)
-
-    for copy in sent + list(g_copies.values()) + list(f_copies.values()):
+            leave((s, h))
+    for copy in sent + list(f_copies.values()):
         copy.wait_send()
 
 

time: 39.6 us -> 43.4 us (1.096)
  Pallas kernels: 36.5 us -> 40.4 us
    pallas_call x1, Pallas kernels: 36.5 us -> 40.4 us  [local(): pl.pallas_call(functools.partial(kernel, rows, cols), out_shape=(jax.Shap...]
where the time goes in v4:
time: 43.4 us; the launch traced here: 43.3 us
  Pallas kernels  40.4 us (93%)
  local copies, waits for them, and re-layouts  2.23 us (5%)
  between operations  0.65 us (1%)
    pallas_call x1, Pallas kernels, local(): pl.pallas_call(functools.partial(kernel, rows, cols), out_shape=(jax.Shap...  40.4 us
    unnamed x4, local copies, waits for them, and re-layouts  2.23 us

profile of v4, /device:TPU:1, one launch (start us, length us, event | category | flops | bytes accessed | tf_op | source)
XLA Modules:
  0.0 43.3 jit_solution(11385163488900579978)
XLA Ops:
  0.6 40.4 %shard_map.104 = (f32[64,512]{1,0:T(8,128)}, f32[64,256]{1,0:T(8,128)}) custom-call(f32[64,512]{1,0:T(8,128)} %stress_in.1, f32[64,256]{1,0:T(8,128)} %state_in.1, s32[64,512]{1,0:T(8,128)} %load_in.1, f32[256]{0:T(256)} %a_hbm.1, f32[256]{0:T(256)} %b_hbm.1, bf16[512,768]{1,0:T(8,128)(2,1)} %band_in.1, bf16[2,4,32,256]{3,2,1,0:T(8,128)(2,1)} %u_in.1, ...), custom_call_target="tpu_custom_call" | custom-call | flops 400000000 | bytes 4000000 | tf_op jit(solution)/shard_map/pallas_call | solution.py:351
  41.0 0.0 copy-start
  41.0 1.6 %copy.13 = f32[64,512]{1,0:T(8,128)} copy(f32[64,512]{1,0:T(8,128)} %get-tuple-element.4) | data formatting | bytes 262144
  42.6 0.0 copy-done
  42.7 0.6 %copy.14 = f32[64,256]{1,0:T(8,128)} copy(f32[64,256]{1,0:T(8,128)S(1)} %copy-done) | data formatting | bytes 131072
Async XLA Ops:
  41.0 1.6 %copy-start = (f32[64,256]{1,0:T(8,128)S(1)}, f32[64,256]{1,0:T(8,128)}, u32[]{:S(2)}) copy-start(f32[64,256]{1,0:T(8,128)} %get-tuple-element.5) | copy-start | bytes 196612

commit v5 on v4

--- a/solution.py
+++ b/solution.py
@@ -285,7 +285,7 @@
         for n in range(3):
             band_t[i, n] = band[i * dofs : (i + 1) * dofs, n * dofs : (n + 1) * dofs].T
     for h in range(halves):
-        for t in order:
+        for t in range(1, chips):
             relay(0, h, t)
     totals = [near_own(0, h) for h in range(halves)]
     for h in range(halves):
@@ -313,7 +313,7 @@
         total = near_own(s, h)
         f_copies[s, h, 0].wait_recv()
         behind = 0
-        for m, t in enumerate(order):
+        for m, t in enumerate(range(1, chips)):
             relay(s, h, t)
             if halves > 1 and m == max(len(order) - 2, 0) and n + 1 < len(turns):
                 leave((s, h))
@@ -344,7 +344,7 @@
     members, own = stress.shape
     block_rows, block_cols, slots, dofs = u_far.shape
     chips = rows // 2
-    halves = 2 if members % 32 == 0 else 1
+    halves = 1
     hbm = pl.BlockSpec(memory_space=pltpu.HBM)
     vmem = pl.BlockSpec(memory_space=pltpu.VMEM)
     dma = pltpu.SemaphoreType.DMA

time: 43.4 us -> 39.8 us (0.917)
  Pallas kernels: 40.4 us -> 36.7 us
    pallas_call x1, Pallas kernels: 40.4 us -> 36.7 us  [local(): pl.pallas_call(functools.partial(kernel, rows, cols), out_shape=(jax.Shap...]
where the time goes in v5:
time: 39.8 us; the launch traced here: 39.6 us
  Pallas kernels  36.7 us (92%)
  local copies, waits for them, and re-layouts  2.23 us (6%)
  between operations  0.65 us (2%)
    pallas_call x1, Pallas kernels, local(): pl.pallas_call(functools.partial(kernel, rows, cols), out_shape=(jax.Shap...  36.7 us
    unnamed x4, local copies, waits for them, and re-layouts  2.23 us

profile of v5, /device:TPU:1, one launch (start us, length us, event | category | flops | bytes accessed | tf_op | source)
XLA Modules:
  0.0 39.6 jit_solution(13311902833540051259)
XLA Ops:
  0.6 36.7 %shard_map.104 = (f32[64,512]{1,0:T(8,128)}, f32[64,256]{1,0:T(8,128)}) custom-call(f32[64,512]{1,0:T(8,128)} %stress_in.1, f32[64,256]{1,0:T(8,128)} %state_in.1, s32[64,512]{1,0:T(8,128)} %load_in.1, f32[256]{0:T(256)} %a_hbm.1, f32[256]{0:T(256)} %b_hbm.1, bf16[512,768]{1,0:T(8,128)(2,1)} %band_in.1, bf16[2,4,32,256]{3,2,1,0:T(8,128)(2,1)} %u_in.1, ...), custom_call_target="tpu_custom_call" | custom-call | flops 400000000 | bytes 4000000 | tf_op jit(solution)/shard_map/pallas_call | solution.py:351
  37.4 0.0 copy-start
  37.4 1.6 %copy.13 = f32[64,512]{1,0:T(8,128)} copy(f32[64,512]{1,0:T(8,128)} %get-tuple-element.4) | data formatting | bytes 262144
  39.0 0.0 copy-done
  39.0 0.6 %copy.14 = f32[64,256]{1,0:T(8,128)} copy(f32[64,256]{1,0:T(8,128)S(1)} %copy-done) | data formatting | bytes 131072
Async XLA Ops:
  37.4 1.6 %copy-start = (f32[64,256]{1,0:T(8,128)S(1)}, f32[64,256]{1,0:T(8,128)}, u32[]{:S(2)}) copy-start(f32[64,256]{1,0:T(8,128)} %get-tuple-element.5) | copy-start | bytes 196612

commit v6 on v3

--- a/solution.py
+++ b/solution.py
@@ -265,12 +265,13 @@
     for h in range(halves):
         excess(0, h)
     mask_u()
+    send_u()
     relay_v()
-    send_u()
     loads[8].wait()
     for i in range(block_rows):
         for n in range(3):
             band_t[i, n] = band[i * dofs : (i + 1) * dofs, n * dofs : (n + 1) * dofs].T
+    relay_u()
     for h in range(halves):
         for t in range(1, chips):
             relay(0, h, t)
@@ -279,7 +280,6 @@
         for t in range(chips):
             f_copies[0, h, t].wait_recv()
         totals[h] = near_edges(0, h, totals[h])
-    relay_u()
     ready = []
     for t in range(cols):
         j = partner(col, t, cols)
@@ -317,6 +317,17 @@
         copy.wait_send()
 
 
+def hand_out(stress_in, state_in, stress_out, state_out, sems):
+    copies = [
+        pltpu.make_async_copy(stress_in, stress_out, sems.at[0]),
+        pltpu.make_async_copy(state_in, state_out, sems.at[1]),
+    ]
+    for copy in copies:
+        copy.start()
+    for copy in copies:
+        copy.wait()
+
+
 def local(stress, state, load_rate, a_param, b_param, near_band, u_far, v_far, ranks):
     rows = lax.axis_size("row")
     cols = lax.axis_size("col")
@@ -327,12 +338,13 @@
     hbm = pl.BlockSpec(memory_space=pltpu.HBM)
     vmem = pl.BlockSpec(memory_space=pltpu.VMEM)
     dma = pltpu.SemaphoreType.DMA
-    return pl.pallas_call(
+    results = (
+        jax.ShapeDtypeStruct(stress.shape, jnp.float32),
+        jax.ShapeDtypeStruct(state.shape, jnp.float32),
+    )
+    stepped = pl.pallas_call(
         functools.partial(kernel, rows, cols),
-        out_shape=(
-            jax.ShapeDtypeStruct(stress.shape, jnp.float32),
-            jax.ShapeDtypeStruct(state.shape, jnp.float32),
-        ),
+        out_shape=results,
         in_specs=[hbm] * 9,
         out_specs=(vmem, vmem),
         scratch_shapes=[
@@ -361,6 +373,16 @@
         ),
         cost_estimate=pl.CostEstimate(flops=400_000_000, bytes_accessed=4_000_000, transcendentals=300_000),
     )(stress, state, load_rate, a_param, b_param, near_band, u_far, v_far, ranks)
+    anywhere = pl.BlockSpec(memory_space=pl.ANY)
+    return pl.pallas_call(
+        hand_out,
+        out_shape=results,
+        in_specs=[anywhere] * 2,
+        out_specs=(anywhere, anywhere),
+        scratch_shapes=[dma((2,))],
+        compiler_params=pltpu.CompilerParams(vmem_limit_bytes=60 * 1024 * 1024),
+        cost_estimate=pl.CostEstimate(flops=0, bytes_accessed=400_000, transcendentals=0),
+    )(*stepped)
 
 
 def solution(mesh):

time: 39.6 us -> 42.3 us (1.068)
  Pallas kernels: 36.5 us -> 41.5 us
  local copies, waits for them, and re-layouts: 2.23 us -> 0 us
    pallas_call x1 -> x2, Pallas kernels: 36.5 us -> 41.5 us  [the longest x1 34.4 us: local(): pl.pallas_call(functools.partial(kernel, rows, cols), out_shape=results,...]
    unnamed x4 -> x0, local copies, waits for them, and re-layouts: 2.23 us -> none
where the time goes in v6:
time: 42.3 us; the launch traced here: 42.1 us
  Pallas kernels  41.5 us (98%)
  between operations  0.64 us (2%)
    pallas_call x1, Pallas kernels, local(): pl.pallas_call(functools.partial(kernel, rows, cols), out_shape=results,...  34.4 us
    pallas_call x1, Pallas kernels, local(): pl.pallas_call(hand_out, out_shape=results, in_specs=[anywhere] * 2, out_...  7.08 us

profile of v6, /device:TPU:1, one launch (start us, length us, event | category | flops | bytes accessed | tf_op | source)
XLA Modules:
  0.0 42.1 jit_solution(9427558598577314128)
XLA Ops:
  0.6 34.4 %shard_map.104 = (f32[64,512]{1,0:T(8,128)}, f32[64,256]{1,0:T(8,128)}) custom-call(f32[64,512]{1,0:T(8,128)} %stress_in.1, f32[64,256]{1,0:T(8,128)} %state_in.1, s32[64,512]{1,0:T(8,128)} %load_in.1, f32[256]{0:T(256)} %a_hbm.1, f32[256]{0:T(256)} %b_hbm.1, bf16[512,768]{1,0:T(8,128)(2,1)} %band_in.1, bf16[2,4,32,256]{3,2,1,0:T(8,128)(2,1)} %u_in.1, ...), custom_call_target="tpu_custom_call" | custom-call | flops 400000000 | bytes 4000000 | tf_op jit(solution)/shard_map/pallas_call | solution.py:345
  35.0 7.1 %shard_map.105 = (f32[64,512]{1,0:T(8,128)}, f32[64,256]{1,0:T(8,128)}) custom-call(f32[64,512]{1,0:T(8,128)} %get-tuple-element.4.stress_in, f32[64,256]{1,0:T(8,128)} %get-tuple-element.5.state_in), custom_call_target="tpu_custom_call" | custom-call | bytes 400000 | tf_op jit(solution)/shard_map/pallas_call | solution.py:377

commit v7 on v6

--- a/solution.py
+++ b/solution.py
@@ -119,11 +119,19 @@
         sent.append(copy)
         return copy
 
-    v_copies = {t: send_factors(0, v_all.at[col], col, t, t) for t in col_steps}
+    v_copies = {}
     u_copies = {}
 
-    def send_u():
-        for t in col_steps:
+    def send_first():
+        for t in [1] if relayed else col_steps:
+            v_copies[t] = send_factors(0, v_all.at[col], col, t, t)
+        if relayed:
+            u_copies[2] = send_factors(1, u_all.at[col], col, 2, 2)
+
+    def send_second():
+        if relayed:
+            v_copies[2] = send_factors(0, v_all.at[col], col, 2, 2)
+        for t in [1] if relayed else col_steps:
             u_copies[t] = send_factors(1, u_all.at[col], col, t, t)
 
     def relay_v():
@@ -260,18 +268,19 @@
                 s, stress0[members_now, lanes], stress_now[members_now, lanes], -total[i]
             )
 
+    mask_u()
+    send_first()
     for copy in loads[3:8]:
         copy.wait()
     for h in range(halves):
         excess(0, h)
-    mask_u()
-    send_u()
+    send_second()
     relay_v()
+    relay_u()
     loads[8].wait()
     for i in range(block_rows):
         for n in range(3):
             band_t[i, n] = band[i * dofs : (i + 1) * dofs, n * dofs : (n + 1) * dofs].T
-    relay_u()
     for h in range(halves):
         for t in range(1, chips):
             relay(0, h, t)
@@ -317,14 +326,17 @@
         copy.wait_send()
 
 
-def hand_out(stress_in, state_in, stress_out, state_out, sems):
-    copies = [
-        pltpu.make_async_copy(stress_in, stress_out, sems.at[0]),
-        pltpu.make_async_copy(state_in, state_out, sems.at[1]),
-    ]
+def hand_out(stress_in, state_in, stress_out, state_out, stress, state, sems):
+    moves = [(stress_in, stress, stress_out), (state_in, state, state_out)]
+    copies = [pltpu.make_async_copy(a, b, sems.at[0, n]) for n, (a, b, _) in enumerate(moves)]
     for copy in copies:
         copy.start()
-    for copy in copies:
+    onward = []
+    for n, (_, b, c) in enumerate(moves):
+        copies[n].wait()
+        onward.append(pltpu.make_async_copy(b, c, sems.at[1, n]))
+        onward[n].start()
+    for copy in onward:
         copy.wait()
 
 
@@ -379,7 +391,11 @@
         out_shape=results,
         in_specs=[anywhere] * 2,
         out_specs=(anywhere, anywhere),
-        scratch_shapes=[dma((2,))],
+        scratch_shapes=[
+            pltpu.VMEM(stress.shape, jnp.float32),
+            pltpu.VMEM(state.shape, jnp.float32),
+            dma((2, 2)),
+        ],
         compiler_params=pltpu.CompilerParams(vmem_limit_bytes=60 * 1024 * 1024),
         cost_estimate=pl.CostEstimate(flops=0, bytes_accessed=400_000, transcendentals=0),
     )(*stepped)

time: 42.3 us -> 35.2 us (0.83)
  Pallas kernels: 41.5 us -> 34.3 us
    pallas_call x1, Pallas kernels: 7.08 us -> 1.61 us  [local(): pl.pallas_call(hand_out, out_shape=results, in_specs=[anywhere] * 2, out_...]
    pallas_call x1, Pallas kernels: 34.4 us -> 32.7 us  [local(): pl.pallas_call(functools.partial(kernel, rows, cols), out_shape=results,...]
where the time goes in v7:
time: 35.2 us; the launch traced here: 35 us
  Pallas kernels  34.3 us (97%)
  between operations  0.64 us (2%)
    pallas_call x1, Pallas kernels, local(): pl.pallas_call(functools.partial(kernel, rows, cols), out_shape=results,...  32.7 us
    pallas_call x1, Pallas kernels, local(): pl.pallas_call(hand_out, out_shape=results, in_specs=[anywhere] * 2, out_...  1.61 us

profile of v7, /device:TPU:1, one launch (start us, length us, event | category | flops | bytes accessed | tf_op | source)
XLA Modules:
  0.0 35.0 jit_solution(6024978542880882230)
XLA Ops:
  0.6 32.7 %shard_map.104 = (f32[64,512]{1,0:T(8,128)}, f32[64,256]{1,0:T(8,128)}) custom-call(f32[64,512]{1,0:T(8,128)} %stress_in.1, f32[64,256]{1,0:T(8,128)} %state_in.1, s32[64,512]{1,0:T(8,128)} %load_in.1, f32[256]{0:T(256)} %a_hbm.1, f32[256]{0:T(256)} %b_hbm.1, bf16[512,768]{1,0:T(8,128)(2,1)} %band_in.1, bf16[2,4,32,256]{3,2,1,0:T(8,128)(2,1)} %u_in.1, ...), custom_call_target="tpu_custom_call" | custom-call | flops 400000000 | bytes 4000000 | tf_op jit(solution)/shard_map/pallas_call | solution.py:357
  33.4 1.6 %shard_map.105 = (f32[64,512]{1,0:T(8,128)}, f32[64,256]{1,0:T(8,128)}) custom-call(f32[64,512]{1,0:T(8,128)} %get-tuple-element.4.stress_in, f32[64,256]{1,0:T(8,128)} %get-tuple-element.5.state_in), custom_call_target="tpu_custom_call" | custom-call | bytes 400000 | tf_op jit(solution)/shard_map/pallas_call | solution.py:389

commit v8 on v7

--- a/solution.py
+++ b/solution.py
@@ -309,11 +309,15 @@
             total = near_own(s, h)
             f_copies[s, h, 0].wait_recv()
             for t in range(1, chips):
-                relay(s, h, t)
+                if (s, h, t) not in f_copies:
+                    relay(s, h, t)
                 if t > 1:
                     f_copies[s, h, t - 1].wait_recv()
                 j = partner(chip, t - 1, chips)
                 total = added(total, far(j, weights(s, h, j)))
+            if h + 1 < halves:
+                for t in range(1, chips - 1):
+                    relay(s, h + 1, t)
             if chips > 1:
                 f_copies[s, h, chips - 1].wait_recv()
             j = partner(chip, chips - 1, chips)

time: 35.2 us -> 36 us (1.023)
  Pallas kernels: 34.3 us -> 35.2 us
    pallas_call x1, Pallas kernels: 32.7 us -> 33.6 us  [local(): pl.pallas_call(functools.partial(kernel, rows, cols), out_shape=results,...]
where the time goes in v8:
time: 36 us; the launch traced here: 35.9 us
  Pallas kernels  35.2 us (98%)
  between operations  0.64 us (2%)
    pallas_call x1, Pallas kernels, local(): pl.pallas_call(functools.partial(kernel, rows, cols), out_shape=results,...  33.6 us
    pallas_call x1, Pallas kernels, local(): pl.pallas_call(hand_out, out_shape=results, in_specs=[anywhere] * 2, out_...  1.61 us

profile of v8, /device:TPU:1, one launch (start us, length us, event | category | flops | bytes accessed | tf_op | source)
XLA Modules:
  0.0 35.9 jit_solution(13051917451568045936)
XLA Ops:
  0.6 33.6 %shard_map.104 = (f32[64,512]{1,0:T(8,128)}, f32[64,256]{1,0:T(8,128)}) custom-call(f32[64,512]{1,0:T(8,128)} %stress_in.1, f32[64,256]{1,0:T(8,128)} %state_in.1, s32[64,512]{1,0:T(8,128)} %load_in.1, f32[256]{0:T(256)} %a_hbm.1, f32[256]{0:T(256)} %b_hbm.1, bf16[512,768]{1,0:T(8,128)(2,1)} %band_in.1, bf16[2,4,32,256]{3,2,1,0:T(8,128)(2,1)} %u_in.1, ...), custom_call_target="tpu_custom_call" | custom-call | flops 400000000 | bytes 4000000 | tf_op jit(solution)/shard_map/pallas_call | solution.py:361
  34.3 1.6 %shard_map.105 = (f32[64,512]{1,0:T(8,128)}, f32[64,256]{1,0:T(8,128)}) custom-call(f32[64,512]{1,0:T(8,128)} %get-tuple-element.4.stress_in, f32[64,256]{1,0:T(8,128)} %get-tuple-element.5.state_in), custom_call_target="tpu_custom_call" | custom-call | bytes 400000 | tf_op jit(solution)/shard_map/pallas_call | solution.py:393
